TPU v7x, 32 devices: a whole 2x2x4 slice. The times are simulated.
32 devices in a mesh: dom: 8 (over z, y), node: 4 (over x, core).
Axes of the slice: x: 2, y: 2, z: 4, core: 2. Of those that a mesh axis runs over, the one named last changes fastest.
Arguments:
- positions: float32 [3, 65536], P(None, ('dom', 'node')), may hold values from -6 to 6
- masses: float32 [65536], P(('dom', 'node')), may hold values from 0.5 to 2
- metric: float32 [6, 65536], P(None, ('dom', 'node')), may hold values from -0.75 to 2.5, as said below
- energy: float32 [65536], P(('dom', 'node')), may hold values from 0.5 to 2
- local_pairs: int32 [512, 1], P(('dom', 'node')), may hold values from 0 to 15
- ghost_pairs: int32 [32, 32], P(('dom', 'node')), may hold values from 0 to 31, each once within a row
- node_sends: int32 [32, 4, 2], P(('dom', 'node')), may hold values from 0 to 15, as said below
- domain_sends: int32 [32, 2, 12], P(('dom', 'node')), may hold values from 0 to 15, as said below
Outputs:
- final_metric: float32 [6, 65536], P(None, ('dom', 'node'))
- density: float32 [65536], P(('dom', 'node'))
- acceleration: float32 [3, 65536], P(None, ('dom', 'node'))
Inputs may be any that keep to these rules, and one draw needn't show every extreme that they name: `local_pairs`: indices of blocks within the owning device. `ghost_pairs`: each device's row names each of its 32 ghost slots exactly once. `node_sends`: indices of blocks within the sending device; each device sends exactly 2 blocks to each device of its node group, itself included, all 8 of them different blocks. `domain_sends`: indices of blocks within the sending device; row 0 goes to the previous domain, row 1 to the next, exactly 12 different blocks in each row. `metric`: each particle's six numbers form a positive definite symmetric matrix.
All inputs are finite; a program needn't handle non-finite values.
Results may differ from a plain program's by a relative error of at most 0.0001.
Values sent between devices are 32-bit elements; how exact they have to be, the bound alone decides.
A program may use at most 64 MiB of HBM per device.

v0:
```python
import jax
import jax.numpy as jnp
from jax import lax
from jax.sharding import PartitionSpec as P

P_SIZE = 128
KL = 1
KG = 2
ITERS = 3


ADIABATIC = 5.0 / 3.0
TARGET_SCALE = 0.5
RIDGE_TERM = 0.1


def padded(cells, sides, width):
    for axis, dim in sides:
        count = lax.axis_size(axis)
        ends = count - 1
        head = lax.slice_in_dim(cells, 0, width, axis=dim)
        tail = lax.slice_in_dim(cells, cells.shape[dim] - width, cells.shape[dim], axis=dim)
        cells = jnp.concatenate(
            [
                lax.ppermute(tail, axis, [(i, (i + 1) % count) for i in range(ends)]),
                cells,
                lax.ppermute(head, axis, [((i + 1) % count, i) for i in range(ends)]),
            ],
            axis=dim,
        )
    return cells


def quad_form(metric, offset):
    return (
        metric[0] * offset[0] * offset[0]
        + metric[1] * offset[1] * offset[1]
        + metric[2] * offset[2] * offset[2]
        + 2.0
        * (
            metric[3] * offset[0] * offset[1]
            + metric[4] * offset[0] * offset[2]
            + metric[5] * offset[1] * offset[2]
        )
    )


def apply_metric(metric, offset):
    return jnp.stack(
        [
            metric[0] * offset[0] + metric[3] * offset[1] + metric[4] * offset[2],
            metric[3] * offset[0] + metric[1] * offset[1] + metric[5] * offset[2],
            metric[4] * offset[0] + metric[5] * offset[1] + metric[2] * offset[2],
        ]
    )


def contract_own(weights, features):
    return jnp.einsum("bij,kbj->kbi", weights, features, precision=lax.Precision.HIGHEST)


def contract_back(weights, features):
    return jnp.einsum("bij,kbi->kbj", weights, features, precision=lax.Precision.HIGHEST)


def moment_features(fields):
    place = fields[0:3]
    mass = fields[3]
    return mass[None] * jnp.stack(
        [
            jnp.ones_like(mass),
            place[0],
            place[1],
            place[2],
            place[0] * place[0],
            place[1] * place[1],
            place[2] * place[2],
            place[0] * place[1],
            place[0] * place[2],
            place[1] * place[2],
        ]
    )


def spread_moments(sums, place):
    total = sums[0]

    def second(first_pos, other_pos, first_sum, other_sum, joint_sum):
        return (
            first_pos * other_pos * total
            - first_pos * other_sum
            - other_pos * first_sum
            + joint_sum
        )

    return jnp.stack(
        [
            total,
            second(place[0], place[0], sums[1], sums[1], sums[4]),
            second(place[1], place[1], sums[2], sums[2], sums[5]),
            second(place[2], place[2], sums[3], sums[3], sums[6]),
            second(place[0], place[1], sums[1], sums[2], sums[7]),
            second(place[0], place[2], sums[1], sums[3], sums[8]),
            second(place[1], place[2], sums[2], sums[3], sums[9]),
        ]
    )


def mass_features(fields):
    mass = fields[3]
    return jnp.stack([mass, mass * fields[0], mass * fields[1], mass * fields[2]])


def force_features(fields):
    scale = 4.0 * fields[3] * fields[10]
    metric = fields[4:10]
    return scale[None] * jnp.concatenate([metric, apply_metric(metric, fields[0:3])], axis=0)


def pair_terms(pass_kind, own_fields, partner_fields):
    offset = own_fields[0:3, :, :, None] - partner_fields[0:3, :, None, :]
    quad_own = 1.0 + quad_form(own_fields[4:10, :, :, None], offset)
    quad_partner = 1.0 + quad_form(partner_fields[4:10, :, None, :], offset)
    own_place = own_fields[0:3]
    partner_place = partner_fields[0:3]
    if pass_kind == "moments":
        weight_own = 1.0 / jnp.square(quad_own)
        weight_partner = 1.0 / jnp.square(quad_partner)
        own_side = spread_moments(
            contract_own(weight_own, moment_features(partner_fields)), own_place
        )
        partner_side = spread_moments(
            contract_back(weight_partner, moment_features(own_fields)), partner_place
        )
    elif pass_kind == "density":
        own_side = contract_own(1.0 / jnp.square(quad_own), partner_fields[3:4])
        partner_side = contract_back(1.0 / jnp.square(quad_partner), own_fields[3:4])
    else:
        cube_own = 1.0 / (quad_own * quad_own * quad_own)
        cube_partner = 1.0 / (quad_partner * quad_partner * quad_partner)
        first = contract_own(cube_own, mass_features(partner_fields))
        term_own = (4.0 * own_fields[10])[None] * apply_metric(
            own_fields[4:10], own_place * first[0:1] - first[1:4]
        )
        second = contract_own(cube_partner, force_features(partner_fields))
        term_cross = apply_metric(second[0:6], own_place) - second[6:9]
        third = contract_back(cube_own, force_features(own_fields))
        term_back = apply_metric(third[0:6], partner_place) - third[6:9]
        fourth = contract_back(cube_partner, mass_features(own_fields))
        term_partner = (4.0 * partner_fields[10])[None] * apply_metric(
            partner_fields[4:10], partner_place * fourth[0:1] - fourth[1:4]
        )
        own_side = term_own + term_cross
        partner_side = term_back + term_partner
    return (own_side, partner_side)


def inverse_parts(matrix):
    cofactors = jnp.stack(
        [
            matrix[1] * matrix[2] - matrix[5] * matrix[5],
            matrix[0] * matrix[2] - matrix[4] * matrix[4],
            matrix[0] * matrix[1] - matrix[3] * matrix[3],
            matrix[4] * matrix[5] - matrix[3] * matrix[2],
            matrix[3] * matrix[5] - matrix[4] * matrix[1],
            matrix[3] * matrix[4] - matrix[0] * matrix[5],
        ]
    )
    determinant = matrix[0] * cofactors[0] + matrix[3] * cofactors[3] + matrix[4] * cofactors[4]
    return (cofactors, determinant)


def next_metric(metric, moment_sums):
    spread = moment_sums[1:] / moment_sums[0]
    ridge_diag = jnp.array([RIDGE_TERM, RIDGE_TERM, RIDGE_TERM, 0.0, 0.0, 0.0], jnp.float32)[
        :, None, None
    ]
    cofactors, determinant = inverse_parts(spread + ridge_diag)
    return 0.5 * metric + 0.5 * TARGET_SCALE * cofactors / determinant


def share_fields(fields, routing):
    node_rows, domain_rows, node_count, node_slots, domain_slots, blocks = routing
    field_count = fields.shape[0]
    node_part = fields[:, node_rows].reshape(field_count, node_count, node_slots, P_SIZE)
    received = lax.all_to_all(node_part, "node", split_axis=1, concat_axis=1, tiled=True)
    extended = padded(fields[:, domain_rows], (("dom", 1),), domain_slots)
    return jnp.concatenate(
        [
            received.reshape(field_count, node_count * node_slots, P_SIZE),
            extended[:, :domain_slots],
            extended[:, 3 * domain_slots :],
        ],
        axis=1,
    )


def send_back(partial_value, routing):
    node_rows, domain_rows, node_count, node_slots, domain_slots, blocks = routing
    field_count = partial_value.shape[0]
    node_part = partial_value[:, : node_count * node_slots].reshape(
        field_count, node_count, node_slots, P_SIZE
    )
    returned = lax.all_to_all(node_part, "node", split_axis=1, concat_axis=1, tiled=True)
    extended = padded(partial_value[:, node_count * node_slots :], (("dom", 1),), domain_slots)
    running = jnp.zeros((field_count, blocks, P_SIZE), jnp.float32)
    running = running.at[:, node_rows].add(
        returned.reshape(field_count, node_count * node_slots, P_SIZE)
    )
    running = running.at[:, domain_rows].add(
        jnp.concatenate([extended[:, :domain_slots], extended[:, 3 * domain_slots :]], axis=1)
    )
    return running


def local_pass(pass_kind, own_fields, ghost_fields, partner, field_count, routing):
    blocks = own_fields.shape[1]
    block_table = jnp.concatenate([own_fields, ghost_fields], axis=1)
    running = jnp.zeros((field_count, block_table.shape[1], P_SIZE), jnp.float32)
    for column in range(partner.shape[1]):
        partner_rows = partner[:, column]
        own_side, partner_side = pair_terms(pass_kind, own_fields, block_table[:, partner_rows])
        running = running.at[:, :blocks].add(own_side)
        running = running.at[:, partner_rows].add(partner_side)
    return running[:, :blocks] + send_back(running[:, blocks:], routing)


def on_device(
    positions, masses, metric, energy, local_pairs, ghost_pairs, node_sends, domain_sends
):
    blocks = local_pairs.shape[0]
    routing = (
        node_sends[0].reshape(-1),
        domain_sends[0].reshape(-1),
        node_sends.shape[1],
        node_sends.shape[2],
        domain_sends.shape[2],
        blocks,
    )
    own_static = jnp.concatenate(
        [positions.reshape(3, blocks, P_SIZE), masses.reshape(1, blocks, P_SIZE)], axis=0
    )
    current_metric = metric.reshape(6, blocks, P_SIZE)
    ghost_first = share_fields(jnp.concatenate([own_static, current_metric], axis=0), routing)
    ghost_static = ghost_first[:4]
    ghost_metric = ghost_first[4:]
    ghost_slots = ghost_pairs[0].reshape(blocks, KG) + blocks
    partner = jnp.concatenate([local_pairs, ghost_slots], axis=1)
    for iteration in range(ITERS):
        own_fields = jnp.concatenate([own_static, current_metric], axis=0)
        ghost_fields = jnp.concatenate([ghost_static, ghost_metric], axis=0)
        moment_sums = local_pass("moments", own_fields, ghost_fields, partner, 7, routing)
        current_metric = next_metric(current_metric, moment_sums)
        ghost_metric = share_fields(current_metric, routing)
    own_fields = jnp.concatenate([own_static, current_metric], axis=0)
    ghost_fields = jnp.concatenate([ghost_static, ghost_metric], axis=0)
    density_sum = local_pass("density", own_fields, ghost_fields, partner, 1, routing)[0]
    cofactors, determinant = inverse_parts(current_metric)
    volume = jnp.sqrt(determinant) / (P_SIZE * (KL + KG))
    density = volume * density_sum
    coefficient = (ADIABATIC - 1.0) * energy.reshape(blocks, P_SIZE) / density * volume
    ghost_coefficient = share_fields(coefficient[None], routing)
    own_fields = jnp.concatenate([own_fields, coefficient[None]], axis=0)
    ghost_fields = jnp.concatenate([ghost_fields, ghost_coefficient], axis=0)
    acceleration = local_pass("force", own_fields, ghost_fields, partner, 3, routing)
    return (current_metric.reshape(6, -1), density.reshape(-1), acceleration.reshape(3, -1))


def solution(mesh):
    in_specs = (
        P(None, ("dom", "node")),
        P(("dom", "node")),
        P(None, ("dom", "node")),
        P(("dom", "node")),
        P(("dom", "node"), None),
        P(("dom", "node"), None),
        P(("dom", "node"), None, None),
        P(("dom", "node"), None, None),
    )
    out_specs = (P(None, ("dom", "node")), P(("dom", "node")), P(None, ("dom", "node")))
    return jax.shard_map(
        on_device, mesh=mesh, in_specs=in_specs, out_specs=out_specs, check_vma=False
    )
```

profile of v0, /device:TPU:26, one launch (start us, length us, event | category | flops | bytes accessed | tf_op | source)
XLA Modules:
  0.0 409.3 jit_solution(5980286798725624456)
XLA Ops:
  37.9 4.9 %convolution_bitcast_fusion.23 = f32[10,16,128]{2,0,1:T(8,128)S(1)} fusion(f32[3,16,128,128]{3,2,1,0:T(8,128)} %copy-done.1, f32[16,128]{1,0:T(8,128)} %bitcast.1327, f32[16,128]{1,0:T(8,128)} %bitcast.1330, f32[16,128]{1,0:T(8,128)S(1)} %bitcast.1318, f32[16,128]{1,0:T(8,128)} %bitcast.1321, f32[16,128]{1,0:T(8,128)} %bitcast.1324, ...), kind=kOutput, calls=%fused_computation.184 | convolution fusion | flops 36982784 | bytes 3366912 | tf_op jit(solution)/shard_map/bij,kbj->kbi/dot_general | solution.py:59
  52.5 4.8 %convolution_bitcast_fusion.21 = f32[10,16,128]{2,0,1:T(8,128)S(1)} fusion(f32[3,16,128,128]{3,2,1,0:T(8,128)} %get-tuple-element.620, f32[16,128]{1,0:T(8,128)} %bitcast.1328, f32[16,128]{1,0:T(8,128)} %bitcast.1331, f32[16,128]{1,0:T(8,128)S(1)} %bitcast.1319, f32[16,128]{1,0:T(8,128)} %bitcast.1322, f32[16,128]{1,0:T(8,128)} %bitcast.1325, ...), kind=kOutput, calls=%fused_computation.182 | convolution fusion | flops 36982784 | bytes 3366912 | tf_op jit(solution)/shard_map/bij,kbj->kbi/dot_general | solution.py:59
  65.3 4.6 %convolution_bitcast_fusion.19 = f32[10,16,128]{2,0,1:T(8,128)S(1)} fusion(f32[3,16,128,128]{3,2,1,0:T(8,128)S(1)} %get-tuple-element.619, f32[16,128]{1,0:T(8,128)S(1)} %bitcast.1329, f32[16,128]{1,0:T(8,128)S(1)} %bitcast.1332, f32[16,128]{1,0:T(8,128)S(1)} %bitcast.1320, f32[16,128]{1,0:T(8,128)S(1)} %bitcast.1323, f32[16,128]{1,0:T(8,128)S(1)} %bitcast.1326, ...), kind=kOutput, calls=%fused_computation.180 | convolution fusion | flops 36982784 | bytes 3366912 | tf_op jit(solution)/shard_map/bij,kbj->kbi/dot_general | solution.py:59
  83.4 4.2 %collective-permute-start.3 = (f32[7,12,128]{2,0,1:T(8,128)S(1)}, f32[7,12,128]{2,0,1:T(8,128)S(1)}, u32[]{:S(2)}, u32[]{:S(2)}) collective-permute-start(f32[7,12,128]{2,0,1:T(8,128)S(1)} %get-tuple-element.273), channel_id=1, source_target_pairs={{4,0},{8,4},{12,8},{16,12},{20,16},{24,20},{28,24},{5,1},{9,5},{13... | collective-permute-start | bytes 129032 | tf_op jit(solution)/shard_map/ppermute | solution.py:27
  100.3 3.9 collective-permute-start.4
  123.2 4.8 %convolution_bitcast_fusion.17 = f32[10,16,128]{2,0,1:T(8,128)S(1)} fusion(f32[3,16,128,128]{3,2,1,0:T(8,128)} %copy-done.2, f32[16,128]{1,0:T(8,128)} %bitcast.1354, f32[16,128]{1,0:T(8,128)} %bitcast.1357, f32[16,128]{1,0:T(8,128)} %bitcast.1360, f32[16,128]{1,0:T(8,128)} %bitcast.1363, f32[16,128]{1,0:T(8,128)} %bitcast.1366, f32[16,128]{1,0:T(8,128)} %bitcast.1351, ...), kind=kOutput, calls=%fused_computation.178 | convolution fusion | flops 36982784 | bytes 3366912 | tf_op jit(solution)/shard_map/bij,kbj->kbi/dot_general | solution.py:59
  137.8 4.8 %convolution_bitcast_fusion.15 = f32[10,16,128]{2,0,1:T(8,128)S(1)} fusion(f32[3,16,128,128]{3,2,1,0:T(8,128)} %get-tuple-element.618, f32[16,128]{1,0:T(8,128)} %bitcast.1355, f32[16,128]{1,0:T(8,128)} %bitcast.1358, f32[16,128]{1,0:T(8,128)} %bitcast.1361, f32[16,128]{1,0:T(8,128)} %bitcast.1364, f32[16,128]{1,0:T(8,128)} %bitcast.1367, ...), kind=kOutput, calls=%fused_computation.176 | convolution fusion | flops 36982784 | bytes 3366912 | tf_op jit(solution)/shard_map/bij,kbj->kbi/dot_general | solution.py:59
  150.5 4.7 %convolution_bitcast_fusion.13 = f32[10,16,128]{2,0,1:T(8,128)S(1)} fusion(f32[3,16,128,128]{3,2,1,0:T(8,128)S(1)} %get-tuple-element.616, f32[16,128]{1,0:T(8,128)} %bitcast.1356, f32[16,128]{1,0:T(8,128)} %bitcast.1359, f32[16,128]{1,0:T(8,128)} %bitcast.1362, f32[16,128]{1,0:T(8,128)} %bitcast.1365, f32[16,128]{1,0:T(8,128)} %bitcast.1368, ...), kind=kOutput, calls=%fused_computation.174 | convolution fusion | flops 36982784 | bytes 3366912 | tf_op jit(solution)/shard_map/bij,kbj->kbi/dot_general | solution.py:59
  161.0 11.5 %scatter_fusion.6 = f32[7,48,128]{2,0,1:T(8,128)S(1)} fusion(f32[7,48,128]{2,0,1:T(8,128)S(1)} %fusion.443, s32[16]{0:T(128)} %copy-done.82, f32[16,7,128]{2,1,0:T(8,128)S(1)} %bitcast.1176), kind=kCustom, calls=%fused_computation.31 | custom fusion | flops 14336 | bytes 172096 | tf_op jit(solution)/shard_map/scatter-add | solution.py:224
  181.2 5.3 %all-to-all-start.3 = ((f32[7,4,2,128]{3,2,0,1:T(2,128)}), f32[7,4,2,128]{3,2,0,1:T(2,128)S(1)}, u32[]{:S(2)}, u32[]{:S(2)}) async-start(f32[7,4,2,128]{3,2,0,1:T(2,128)} %copy.114), calls=%async_computation.3 | async-start | bytes 57344 | tf_op jit(solution)/shard_map/all_to_all | solution.py:204
  199.3 5.2 %all-to-all-start.4 = ((f32[6,4,2,128]{3,2,0,1:T(2,128)}), f32[6,4,2,128]{3,2,0,1:T(2,128)S(1)}, u32[]{:S(2)}, u32[]{:S(2)}) async-start(f32[6,4,2,128]{3,2,0,1:T(2,128)} %copy.117), calls=%async_computation.4 | async-start | bytes 49152 | tf_op jit(solution)/shard_map/all_to_all | solution.py:186
  220.9 4.8 %convolution_bitcast_fusion.11 = f32[10,16,128]{2,0,1:T(8,128)S(1)} fusion(f32[3,16,128,128]{3,2,1,0:T(8,128)} %copy-done.3, f32[16,128]{1,0:T(8,128)} %bitcast.1336, f32[16,128]{1,0:T(8,128)} %bitcast.1339, f32[16,128]{1,0:T(8,128)} %bitcast.1342, f32[16,128]{1,0:T(8,128)} %bitcast.1345, f32[16,128]{1,0:T(8,128)} %bitcast.1348, f32[16,128]{1,0:T(8,128)} %bitcast.1333, ...), kind=kOutput, calls=%fused_computation.172 | convolution fusion | flops 36982784 | bytes 3366912 | tf_op jit(solution)/shard_map/bij,kbj->kbi/dot_general | solution.py:59
  236.9 4.8 %convolution_bitcast_fusion.9 = f32[10,16,128]{2,0,1:T(8,128)S(1)} fusion(f32[3,16,128,128]{3,2,1,0:T(8,128)} %get-tuple-element.615, f32[16,128]{1,0:T(8,128)} %bitcast.1337, f32[16,128]{1,0:T(8,128)} %bitcast.1340, f32[16,128]{1,0:T(8,128)} %bitcast.1343, f32[16,128]{1,0:T(8,128)} %bitcast.1346, f32[16,128]{1,0:T(8,128)} %bitcast.1349, ...), kind=kOutput, calls=%fused_computation.170 | convolution fusion | flops 36982784 | bytes 3366912 | tf_op jit(solution)/shard_map/bij,kbj->kbi/dot_general | solution.py:59
  249.9 5.5 %convolution_bitcast_fusion.7 = f32[10,16,128]{2,0,1:T(8,128)S(1)} fusion(f32[3,16,128,128]{3,2,1,0:T(8,128)S(1)} %get-tuple-element.613, f32[16,128]{1,0:T(8,128)} %bitcast.1338, f32[16,128]{1,0:T(8,128)} %bitcast.1341, f32[16,128]{1,0:T(8,128)} %bitcast.1344, f32[16,128]{1,0:T(8,128)} %bitcast.1347, f32[16,128]{1,0:T(8,128)} %bitcast.1350, ...), kind=kOutput, calls=%fused_computation.168 | convolution fusion | flops 36982784 | bytes 3366912 | tf_op jit(solution)/shard_map/bij,kbj->kbi/dot_general | solution.py:59
  265.8 5.2 %all-to-all-start.5 = ((f32[7,4,2,128]{3,2,0,1:T(2,128)}), f32[7,4,2,128]{3,2,0,1:T(2,128)S(1)}, u32[]{:S(2)}, u32[]{:S(2)}) async-start(f32[7,4,2,128]{3,2,0,1:T(2,128)} %copy.122), calls=%async_computation.5 | async-start | bytes 57344 | tf_op jit(solution)/shard_map/all_to_all | solution.py:204
  271.0 4.6 %collective-permute-start.11 = (f32[7,12,128]{2,0,1:T(8,128)S(1)}, f32[7,12,128]{2,0,1:T(8,128)S(1)}, u32[]{:S(2)}, u32[]{:S(2)}) collective-permute-start(f32[7,12,128]{2,0,1:T(8,128)S(1)} %get-tuple-element.269), channel_id=1, source_target_pairs={{4,0},{8,4},{12,8},{16,12},{20,16},{24,20},{28,24},{5,1},{9,5},{13... | collective-permute-start | bytes 129032 | tf_op jit(solution)/shard_map/ppermute | solution.py:27
  286.6 3.8 collective-permute-start.13
  311.1 4.8 %fusion.198 = f32[16,1,128]{2,1,0:T(1,128)S(1)} fusion(f32[3,16,128,128]{3,2,1,0:T(8,128)} %get-tuple-element.612, f32[16,128]{1,0:T(8,128)S(1)} %bitcast.1196, f32[16,128]{1,0:T(8,128)S(1)} %bitcast.1217, f32[16,128]{1,0:T(8,128)S(1)} %bitcast.1189, f32[16,128]{1,0:T(8,128)S(1)} %bitcast.1203, f32[16,128]{1,0:T(8,128)S(1)} %bitcast.1210, ...), kind=kOutput, calls=%fused_computation.413 | convolution fusion | flops 8650752 | bytes 3211264 | tf_op jit(solution)/shard_map/bij,kbj->kbi/dot_general | solution.py:59
  320.3 4.3 %fusion.194 = f32[16,1,128]{2,1,0:T(1,128)S(1)} fusion(f32[3,16,128,128]{3,2,1,0:T(8,128)S(1)} %get-tuple-element.610, f32[16,128]{1,0:T(8,128)S(1)} %bitcast.1197, f32[16,128]{1,0:T(8,128)S(1)} %bitcast.1218, f32[16,128]{1,0:T(8,128)S(1)} %bitcast.1190, f32[16,128]{1,0:T(8,128)S(1)} %bitcast.1204, f32[16,128]{1,0:T(8,128)S(1)} %bitcast.1211, ...), kind=kOutput, calls=%fused_computation.411 | convolution fusion | flops 8650752 | bytes 3211264 | tf_op jit(solution)/shard_map/bij,kbj->kbi/dot_general | solution.py:59
  328.5 5.2 %all-to-all-start.7 = ((f32[1,4,2,128]{3,2,0,1:T(2,128)}), f32[1,4,2,128]{3,2,0,1:T(2,128)S(1)}, u32[]{:S(2)}, u32[]{:S(2)}) async-start(f32[1,4,2,128]{3,2,0,1:T(2,128)} %bitcast.286), calls=%async_computation.7 | async-start | bytes 8192 | tf_op jit(solution)/shard_map/all_to_all | solution.py:204
  333.7 4.7 %collective-permute-start.15 = (f32[1,12,128]{2,1,0:T(8,128)S(1)}, f32[1,12,128]{2,1,0:T(8,128)S(1)}, u32[]{:S(2)}, u32[]{:S(2)}) collective-permute-start(f32[1,12,128]{2,1,0:T(8,128)S(1)} %get-tuple-element.609), channel_id=1, source_target_pairs={{4,0},{8,4},{12,8},{16,12},{20,16},{24,20},{28,24},{5,1},{9,5},{13... | collective-permute-start | bytes 18440 | tf_op jit(solution)/shard_map/ppermute | solution.py:27
  341.1 3.8 collective-permute-done.14
  349.6 3.9 collective-permute-start.16
  392.1 5.2 %all-to-all-start.9 = ((f32[3,4,2,128]{3,2,0,1:T(2,128)}), f32[3,4,2,128]{3,2,0,1:T(2,128)S(1)}, u32[]{:S(2)}, u32[]{:S(2)}) async-start(f32[3,4,2,128]{3,2,0,1:T(2,128)} %copy.135), calls=%async_computation.9 | async-start | bytes 24576 | tf_op jit(solution)/shard_map/all_to_all | solution.py:204
  (659 shorter events, 285.8 us)
Async XLA Ops:
  2.9 21.4 %collective-permute-start.1 = (f32[10,12,128]{2,0,1:T(8,128)S(1)}, f32[10,12,128]{2,0,1:T(8,128)S(1)}, u32[]{:S(2)}, u32[]{:S(2)}) collective-permute-start(f32[10,12,128]{2,0,1:T(8,128)S(1)} %get-tuple-element.275), channel_id=1, source_target_pairs={{4,0},{8,4},{12,8},{16,12},{20,16},{24,20},{28,24},{5,1},{9,5},{13... | collective-permute-start | bytes 184328 | tf_op jit(solution)/shard_map/ppermute | solution.py:27
  6.2 18.1 %collective-permute-start = (f32[10,12,128]{2,0,1:T(8,128)S(1)}, f32[10,12,128]{2,0,1:T(8,128)S(1)}, u32[]{:S(2)}, u32[]{:S(2)}) collective-permute-start(f32[10,12,128]{2,0,1:T(8,128)S(1)} %get-tuple-element.274), channel_id=1, source_target_pairs={{0,4},{4,8},{8,12},{12,16},{16,20},{20,24},{24,28},{1,5},{5,9},{9,... | collective-permute-start | bytes 184328 | tf_op jit(solution)/shard_map/ppermute | solution.py:25
  10.9 13.5 %all-to-all-start = ((f32[10,4,2,128]{3,2,0,1:T(2,128)}), f32[10,4,2,128]{3,2,0,1:T(2,128)S(1)}, u32[]{:S(2)}, u32[]{:S(2)}) async-start(f32[10,4,2,128]{3,2,0,1:T(2,128)} %copy.95), calls=%async_computation | async-start | bytes 81920 | tf_op jit(solution)/shard_map/all_to_all | solution.py:186
  80.1 10.3 %all-to-all-start.1 = ((f32[7,4,2,128]{3,2,0,1:T(2,128)}), f32[7,4,2,128]{3,2,0,1:T(2,128)S(1)}, u32[]{:S(2)}, u32[]{:S(2)}) async-start(f32[7,4,2,128]{3,2,0,1:T(2,128)} %copy.106), calls=%async_computation.1 | async-start | bytes 57344 | tf_op jit(solution)/shard_map/all_to_all | solution.py:204
  83.4 7.8 %collective-permute-start.3 = (f32[7,12,128]{2,0,1:T(8,128)S(1)}, f32[7,12,128]{2,0,1:T(8,128)S(1)}, u32[]{:S(2)}, u32[]{:S(2)}) collective-permute-start(f32[7,12,128]{2,0,1:T(8,128)S(1)} %get-tuple-element.273), channel_id=1, source_target_pairs={{4,0},{8,4},{12,8},{16,12},{20,16},{24,20},{28,24},{5,1},{9,5},{13... | collective-permute-start | bytes 129032 | tf_op jit(solution)/shard_map/ppermute | solution.py:27
  98.4 11.7 %collective-permute-start.5 = (f32[6,12,128]{2,0,1:T(8,128)S(1)}, f32[6,12,128]{2,0,1:T(8,128)S(1)}, u32[]{:S(2)}, u32[]{:S(2)}) collective-permute-start(f32[6,12,128]{2,0,1:T(8,128)S(1)} %get-tuple-element.556), channel_id=1, source_target_pairs={{4,0},{8,4},{12,8},{16,12},{20,16},{24,20},{28,24},{5,1},{9,5},{13... | collective-permute-start | bytes 110600 | tf_op jit(solution)/shard_map/ppermute | solution.py:27
  100.3 9.8 %collective-permute-start.4 = (f32[6,12,128]{2,0,1:T(8,128)S(1)}, f32[6,12,128]{2,0,1:T(8,128)S(1)}, u32[]{:S(2)}, u32[]{:S(2)}) collective-permute-start(f32[6,12,128]{2,0,1:T(8,128)S(1)} %get-tuple-element.555), channel_id=1, source_target_pairs={{0,4},{4,8},{8,12},{12,16},{16,20},{20,24},{24,28},{1,5},{5,9},{9,... | collective-permute-start | bytes 110600 | tf_op jit(solution)/shard_map/ppermute | solution.py:25
  174.7 14.6 %collective-permute-start.7 = (f32[7,12,128]{2,0,1:T(8,128)S(1)}, f32[7,12,128]{2,0,1:T(8,128)S(1)}, u32[]{:S(2)}, u32[]{:S(2)}) collective-permute-start(f32[7,12,128]{2,0,1:T(8,128)S(1)} %get-tuple-element.271), channel_id=1, source_target_pairs={{4,0},{8,4},{12,8},{16,12},{20,16},{24,20},{28,24},{5,1},{9,5},{13... | collective-permute-start | bytes 129032 | tf_op jit(solution)/shard_map/ppermute | solution.py:27
  177.5 11.8 %collective-permute-start.6 = (f32[7,12,128]{2,0,1:T(8,128)S(1)}, f32[7,12,128]{2,0,1:T(8,128)S(1)}, u32[]{:S(2)}, u32[]{:S(2)}) collective-permute-start(f32[7,12,128]{2,0,1:T(8,128)S(1)} %get-tuple-element.270), channel_id=1, source_target_pairs={{0,4},{4,8},{8,12},{12,16},{16,20},{20,24},{24,28},{1,5},{5,9},{9,... | collective-permute-start | bytes 129032 | tf_op jit(solution)/shard_map/ppermute | solution.py:25
  181.2 7.2 %all-to-all-start.3 = ((f32[7,4,2,128]{3,2,0,1:T(2,128)}), f32[7,4,2,128]{3,2,0,1:T(2,128)S(1)}, u32[]{:S(2)}, u32[]{:S(2)}) async-start(f32[7,4,2,128]{3,2,0,1:T(2,128)} %copy.114), calls=%async_computation.3 | async-start | bytes 57344 | tf_op jit(solution)/shard_map/all_to_all | solution.py:204
  192.9 13.6 %collective-permute-start.9 = (f32[6,12,128]{2,0,1:T(8,128)S(1)}, f32[6,12,128]{2,0,1:T(8,128)S(1)}, u32[]{:S(2)}, u32[]{:S(2)}) collective-permute-start(f32[6,12,128]{2,0,1:T(8,128)S(1)} %get-tuple-element.554), channel_id=1, source_target_pairs={{4,0},{8,4},{12,8},{16,12},{20,16},{24,20},{28,24},{5,1},{9,5},{13... | collective-permute-start | bytes 110600 | tf_op jit(solution)/shard_map/ppermute | solution.py:27
  196.6 9.9 %collective-permute-start.8 = (f32[6,12,128]{2,0,1:T(8,128)S(1)}, f32[6,12,128]{2,0,1:T(8,128)S(1)}, u32[]{:S(2)}, u32[]{:S(2)}) collective-permute-start(f32[6,12,128]{2,0,1:T(8,128)S(1)} %get-tuple-element.553), channel_id=1, source_target_pairs={{0,4},{4,8},{8,12},{12,16},{16,20},{20,24},{24,28},{1,5},{5,9},{9,... | collective-permute-start | bytes 110600 | tf_op jit(solution)/shard_map/ppermute | solution.py:25
  199.3 7.1 %all-to-all-start.4 = ((f32[6,4,2,128]{3,2,0,1:T(2,128)}), f32[6,4,2,128]{3,2,0,1:T(2,128)S(1)}, u32[]{:S(2)}, u32[]{:S(2)}) async-start(f32[6,4,2,128]{3,2,0,1:T(2,128)} %copy.117), calls=%async_computation.4 | async-start | bytes 49152 | tf_op jit(solution)/shard_map/all_to_all | solution.py:186
  265.8 14.8 %all-to-all-start.5 = ((f32[7,4,2,128]{3,2,0,1:T(2,128)}), f32[7,4,2,128]{3,2,0,1:T(2,128)S(1)}, u32[]{:S(2)}, u32[]{:S(2)}) async-start(f32[7,4,2,128]{3,2,0,1:T(2,128)} %copy.122), calls=%async_computation.5 | async-start | bytes 57344 | tf_op jit(solution)/shard_map/all_to_all | solution.py:204
  271.0 10.5 %collective-permute-start.11 = (f32[7,12,128]{2,0,1:T(8,128)S(1)}, f32[7,12,128]{2,0,1:T(8,128)S(1)}, u32[]{:S(2)}, u32[]{:S(2)}) collective-permute-start(f32[7,12,128]{2,0,1:T(8,128)S(1)} %get-tuple-element.269), channel_id=1, source_target_pairs={{4,0},{8,4},{12,8},{16,12},{20,16},{24,20},{28,24},{5,1},{9,5},{13... | collective-permute-start | bytes 129032 | tf_op jit(solution)/shard_map/ppermute | solution.py:27
  275.7 6.9 %collective-permute-start.10 = (f32[7,12,128]{2,0,1:T(8,128)S(1)}, f32[7,12,128]{2,0,1:T(8,128)S(1)}, u32[]{:S(2)}, u32[]{:S(2)}) collective-permute-start(f32[7,12,128]{2,0,1:T(8,128)S(1)} %get-tuple-element.268), channel_id=1, source_target_pairs={{0,4},{4,8},{8,12},{12,16},{16,20},{20,24},{24,28},{1,5},{5,9},{9,... | collective-permute-start | bytes 129032 | tf_op jit(solution)/shard_map/ppermute | solution.py:25
  286.6 11.7 %collective-permute-start.13 = (f32[6,12,128]{2,0,1:T(8,128)S(1)}, f32[6,12,128]{2,0,1:T(8,128)S(1)}, u32[]{:S(2)}, u32[]{:S(2)}) collective-permute-start(f32[6,12,128]{2,0,1:T(8,128)S(1)} %get-tuple-element.552), channel_id=1, source_target_pairs={{4,0},{8,4},{12,8},{16,12},{20,16},{24,20},{28,24},{5,1},{9,5},{13... | collective-permute-start | bytes 110600 | tf_op jit(solution)/shard_map/ppermute | solution.py:27
  290.5 7.8 %collective-permute-start.12 = (f32[6,12,128]{2,0,1:T(8,128)S(1)}, f32[6,12,128]{2,0,1:T(8,128)S(1)}, u32[]{:S(2)}, u32[]{:S(2)}) collective-permute-start(f32[6,12,128]{2,0,1:T(8,128)S(1)} %get-tuple-element.551), channel_id=1, source_target_pairs={{0,4},{4,8},{8,12},{12,16},{16,20},{20,24},{24,28},{1,5},{5,9},{9,... | collective-permute-start | bytes 110600 | tf_op jit(solution)/shard_map/ppermute | solution.py:25
  328.5 11.9 %all-to-all-start.7 = ((f32[1,4,2,128]{3,2,0,1:T(2,128)}), f32[1,4,2,128]{3,2,0,1:T(2,128)S(1)}, u32[]{:S(2)}, u32[]{:S(2)}) async-start(f32[1,4,2,128]{3,2,0,1:T(2,128)} %bitcast.286), calls=%async_computation.7 | async-start | bytes 8192 | tf_op jit(solution)/shard_map/all_to_all | solution.py:204
  333.7 7.3 %collective-permute-start.15 = (f32[1,12,128]{2,1,0:T(8,128)S(1)}, f32[1,12,128]{2,1,0:T(8,128)S(1)}, u32[]{:S(2)}, u32[]{:S(2)}) collective-permute-start(f32[1,12,128]{2,1,0:T(8,128)S(1)} %get-tuple-element.609), channel_id=1, source_target_pairs={{4,0},{8,4},{12,8},{16,12},{20,16},{24,20},{28,24},{5,1},{9,5},{13... | collective-permute-start | bytes 18440 | tf_op jit(solution)/shard_map/ppermute | solution.py:27
  347.7 10.9 %collective-permute-start.17 = (f32[1,12,128]{2,0,1:T(1,128)S(1)}, f32[1,12,128]{2,0,1:T(1,128)S(1)}, u32[]{:S(2)}, u32[]{:S(2)}) collective-permute-start(f32[1,12,128]{2,0,1:T(1,128)S(1)} %get-tuple-element.623), channel_id=1, source_target_pairs={{4,0},{8,4},{12,8},{16,12},{20,16},{24,20},{28,24},{5,1},{9,5},{13... | collective-permute-start | bytes 18440 | tf_op jit(solution)/shard_map/ppermute | solution.py:27
  349.6 9.0 %collective-permute-start.16 = (f32[1,12,128]{2,0,1:T(1,128)S(1)}, f32[1,12,128]{2,0,1:T(1,128)S(1)}, u32[]{:S(2)}, u32[]{:S(2)}) collective-permute-start(f32[1,12,128]{2,0,1:T(1,128)S(1)} %get-tuple-element.622), channel_id=1, source_target_pairs={{0,4},{4,8},{8,12},{12,16},{16,20},{20,24},{24,28},{1,5},{5,9},{9,... | collective-permute-start | bytes 18440 | tf_op jit(solution)/shard_map/ppermute | solution.py:25
  392.1 11.7 %all-to-all-start.9 = ((f32[3,4,2,128]{3,2,0,1:T(2,128)}), f32[3,4,2,128]{3,2,0,1:T(2,128)S(1)}, u32[]{:S(2)}, u32[]{:S(2)}) async-start(f32[3,4,2,128]{3,2,0,1:T(2,128)} %copy.135), calls=%async_computation.9 | async-start | bytes 24576 | tf_op jit(solution)/shard_map/all_to_all | solution.py:204
  397.3 7.3 %collective-permute-start.19 = (f32[3,12,128]{2,0,1:T(4,128)S(1)}, f32[3,12,128]{2,0,1:T(4,128)S(1)}, u32[]{:S(2)}, u32[]{:S(2)}) collective-permute-start(f32[3,12,128]{2,0,1:T(4,128)S(1)} %get-tuple-element.538), channel_id=1, source_target_pairs={{4,0},{8,4},{12,8},{16,12},{20,16},{24,20},{28,24},{5,1},{9,5},{13... | collective-permute-start | bytes 55304 | tf_op jit(solution)/shard_map/ppermute | solution.py:27
  (137 other events, 1093.2 us)
where the time goes:
time: 418 us; the launch traced here: 409 us
  starting transfers between devices  103 us (25%)
  other arithmetic  102 us (24%)
  matrix products  101 us (24%)
  local copies, waits for them, and re-layouts  81.4 us (19%)
  waiting for transfers between devices  17.5 us (4%)
    dot_general x18, matrix products, contract_own(): jnp.einsum('bij,kbj->kbi', weights, features, precision=lax.Precision.HIG...  67 us
    dot_general x18, matrix products, contract_back(): jnp.einsum('bij,kbi->kbj', weights, features, precision=lax.Precision.HIG...  34 us
    ppermute x10, starting transfers between devices, padded(): lax.ppermute(head, axis, [((i + 1) % count, i) for i in range(ends)])  33.9 us
    scatter-add x15, other arithmetic, local_pass(): running = running.at[:, partner_rows].add(partner_side)  27.3 us
    add x36, other arithmetic, second(): first_pos * other_pos * total - first_pos * other_sum  26.8 us
    ppermute x10, starting transfers between devices, padded(): lax.ppermute(tail, axis, [(i, (i + 1) % count) for i in range(ends)])  26.3 us
    all_to_all x5, starting transfers between devices, send_back(): lax.all_to_all(node_part, 'node', split_axis=1, concat_axis=1, tiled=True)  24.3 us
    all_to_all x5, starting transfers between devices, share_fields(): lax.all_to_all(node_part, 'node', split_axis=1, concat_axis=1, tiled=True)  18.9 us
  transfers between devices with their start and end apart: 30, of which 9 were waited for; matrix products, arithmetic and copies ran while one was open for 6% of the time, Pallas kernels for 0%

commit v1 on v0

v1 whole, which is shorter than its diff:
```python
import functools

import jax
import jax.numpy as jnp
from jax import lax
from jax.experimental import pallas as pl
from jax.experimental.pallas import tpu as pltpu
from jax.sharding import PartitionSpec as P

SIZE = 128
KG = 2
LISTED = 3
ITERS = 3
STEPS = 8
AHEAD = 2
ADIABATIC = 5.0 / 3.0
TARGET_SCALE = 0.5
RIDGE_TERM = 0.1
TERMS = 10
HALF = 64
MESH = pl.DeviceIdType.MESH
F32 = jnp.float32
BF16 = jnp.bfloat16


def lanes(block, count=1):
    return pl.ds(pl.multiple_of(block * SIZE, SIZE), count * SIZE)


def greet(n_dom, n_node):
    a, c = lax.axis_index("dom"), lax.axis_index("node")
    barrier = pltpu.get_barrier_semaphore()
    for turn in range(1, n_node):
        pl.semaphore_signal(
            barrier, inc=1, device_id=(a, lax.rem(c + turn, n_node)), device_id_type=MESH
        )

    @pl.when(a > 0)
    def _():
        pl.semaphore_signal(barrier, inc=1, device_id=(a - 1, c), device_id_type=MESH)

    @pl.when(a < n_dom - 1)
    def _():
        pl.semaphore_signal(barrier, inc=1, device_id=(a + 1, c), device_id_type=MESH)

    inner = (a > 0).astype(jnp.int32) + (a < n_dom - 1).astype(jnp.int32)
    pl.semaphore_wait(barrier, n_node - 1 + inner)


def static_exchange(
    n_dom, n_node, pos_ref, mass_ref, node_ref, domain_ref, ghost_ref, recv_ref, rtab_ref, send, land
):
    a, c = lax.axis_index("dom"), lax.axis_index("node")
    prev_slot, next_slot = n_node, n_node + 1
    recv_ref[c, 0:3, :] = pos_ref[...]
    recv_ref[c, 3:4, :] = mass_ref[...]
    rtab_ref[c] = jnp.zeros(rtab_ref.shape[1:], jnp.int32)
    capn = node_ref.shape[1]
    rtab_ref[c, 0:capn, 0:n_node] = node_ref[0]
    rtab_ref[c, capn:capn + 2, 0:domain_ref.shape[2]] = domain_ref[0]
    rtab_ref[c, capn + 2:capn + 3, 0:ghost_ref.shape[1]] = ghost_ref[...]

    @pl.when(a == 0)
    def _():
        recv_ref[prev_slot] = jnp.zeros(recv_ref.shape[1:], F32)
        rtab_ref[prev_slot] = jnp.zeros(rtab_ref.shape[1:], jnp.int32)

    @pl.when(a == n_dom - 1)
    def _():
        recv_ref[next_slot] = jnp.zeros(recv_ref.shape[1:], F32)
        rtab_ref[next_slot] = jnp.zeros(rtab_ref.shape[1:], jnp.int32)

    greet(n_dom, n_node)

    def copies(lane, target, slot):
        return [
            pltpu.make_async_remote_copy(
                src_ref=ref.at[c],
                dst_ref=ref.at[slot],
                send_sem=send.at[lane, part],
                recv_sem=land.at[lane, part],
                device_id=target,
                device_id_type=MESH,
            )
            for part, ref in enumerate((recv_ref, rtab_ref))
        ]

    to_prev = copies(0, (a - 1, c), next_slot)
    to_next = copies(1, (a + 1, c), prev_slot)
    around = [
        copies(1 + turn, (a, lax.rem(c + turn, n_node)), c) for turn in range(1, n_node)
    ]
    finish(a, n_dom, to_prev, to_next, around)


def finish(a, n_dom, to_prev, to_next, around):
    @pl.when(a > 0)
    def _():
        for copy in to_prev:
            copy.start()

    @pl.when(a < n_dom - 1)
    def _():
        for copy in to_next:
            copy.start()

    for group in around:
        for copy in group:
            copy.start()
    for group in around:
        for copy in group:
            copy.wait()

    @pl.when(a > 0)
    def _():
        for copy in to_prev:
            copy.wait_send()
        for copy in to_next:
            copy.wait_recv()

    @pl.when(a < n_dom - 1)
    def _():
        for copy in to_next:
            copy.wait_send()
        for copy in to_prev:
            copy.wait_recv()


def term_exchange(n_dom, n_node, capn, capd, pay_ref, recv_ref, send, land):
    a, c = lax.axis_index("dom"), lax.axis_index("node")
    first = n_node * capn
    prev_cols = pl.ds(first * SIZE, capd * SIZE)
    next_cols = pl.ds((first + capd) * SIZE, capd * SIZE)
    recv_ref[:, lanes(c * capn, capn)] = pay_ref[:, lanes(c * capn, capn)]

    @pl.when(a == 0)
    def _():
        recv_ref[:, prev_cols] = jnp.zeros((8, capd * SIZE), F32)

    @pl.when(a == n_dom - 1)
    def _():
        recv_ref[:, next_cols] = jnp.zeros((8, capd * SIZE), F32)

    greet(n_dom, n_node)

    def copies(lane, target, src, dst):
        return [
            pltpu.make_async_remote_copy(
                src_ref=pay_ref.at[:, src],
                dst_ref=recv_ref.at[:, dst],
                send_sem=send.at[lane],
                recv_sem=land.at[lane],
                device_id=target,
                device_id_type=MESH,
            )
        ]

    to_prev = copies(0, (a - 1, c), prev_cols, next_cols)
    to_next = copies(1, (a + 1, c), next_cols, prev_cols)
    around = []
    for turn in range(1, n_node):
        peer = lax.rem(c + turn, n_node)
        around.append(copies(1 + turn, (a, peer), lanes(peer * capn, capn), lanes(c * capn, capn)))
    finish(a, n_dom, to_prev, to_next, around)


def set_parts(out, base, values, order):
    count = values[0].shape[0]
    for k, value in enumerate(values):
        high = value.astype(BF16).astype(F32)
        rest = value - high
        middle = rest.astype(BF16).astype(F32)
        parts = (high, middle, rest - middle)
        for group, part in enumerate(order):
            at = base + (TERMS * group + k) * count
            out[at:at + count, :] = parts[part]


def split2(value):
    high = value.astype(BF16)
    return high, (value - high.astype(F32)).astype(BF16)


def dot(left, right):
    return jnp.dot(left, right, preferred_element_type=F32)


def inverse_parts(m):
    cofactors = [
        m[1] * m[2] - m[5] * m[5],
        m[0] * m[2] - m[4] * m[4],
        m[0] * m[1] - m[3] * m[3],
        m[4] * m[5] - m[3] * m[2],
        m[3] * m[5] - m[4] * m[1],
        m[3] * m[4] - m[0] * m[5],
    ]
    return cofactors, m[0] * cofactors[0] + m[3] * cofactors[3] + m[4] * cofactors[4]


def apply_metric(m, x):
    return [
        m[0] * x[0] + m[3] * x[1] + m[4] * x[2],
        m[3] * x[0] + m[1] * x[1] + m[5] * x[2],
        m[4] * x[0] + m[5] * x[1] + m[2] * x[2],
    ]


def inverse_of(s):
    return pltpu.reciprocal(s, approx=True)


def compute(
    sizes,
    tab_ref, local_ref, recv_ref, metric_ref, energy_ref,
    final_ref, density_ref, accel_ref, pay_ref,
    held, src, pack, low_t, high_t, twin_t, feat_m, narrow, coef, acc, thirds_acc, cubes, back_feat, backs, own,
):
    n_node, capn, capd, blocks = sizes
    ghosts = blocks * KG
    sources = blocks + 2 * ghosts
    first = n_node * capn
    ghost_row = capn + 2
    slots = n_node + 2
    c = lax.axis_index("node")

    def strided(n, count, stride):
        return pl.ds(n, count, stride=stride)

    for slot in range(slots):
        if slot >= n_node:
            @pl.loop(0, ghosts, unroll=8)
            def _(n, slot=slot):
                held[slot, n] = 0

        @pl.loop(0, ghosts, unroll=8)
        def _(n, slot=slot):
            held[slot, tab_ref[slot, ghost_row, n]] = n // KG

    for n in range(blocks):
        at = slice(n * SIZE, (n + 1) * SIZE)
        src[strided(n, 4, sources), :] = recv_ref[c, :, at]
        own[strided(n, 6, blocks), :] = metric_ref[:, at]
        own[6 * blocks + n:6 * blocks + n + 1, :] = energy_ref[:, at]

    for n in range(ghosts):
        slot = tab_ref[c, ghost_row, n]
        near = slot < first
        low = slot < first + capd
        past = slot - first
        from_slot = jnp.where(near, slot // capn, jnp.where(low, n_node, n_node + 1))
        row = jnp.where(near, slot % capn, jnp.where(low, capn + 1, capn))
        col = jnp.where(near, c, jnp.where(low, past, past - capd))
        block = tab_ref[from_slot, row, col]
        src[strided(blocks + n, 4, sources), :] = recv_ref[from_slot, :, lanes(block)]

    for n in range(ghosts):
        if n < first:
            from_slot, there = n // capn, c * capn + n % capn
        elif n < first + capd:
            from_slot, there = n_node, n + capd
        else:
            from_slot, there = n_node + 1, n - capd
        block = held[from_slot, there]
        src[strided(blocks + ghosts + n, 4, sources), :] = recv_ref[from_slot, :, lanes(block)]

    def send_target(n):
        near = n < first
        low = n < first + capd
        past = n - first
        row = jnp.where(near, n % capn, jnp.where(low, capn, capn + 1))
        return tab_ref[c, row, jnp.where(near, n // capn, jnp.where(low, past, past - capd))]

    x, y, z, mass = (src[k * sources:(k + 1) * sources, :] for k in range(4))
    feature = [jnp.ones_like(x), x, y, z, x * x, y * y, z * z, x * y, x * z, y * z]
    pack[60 * sources:, :] = jnp.zeros((4 * sources, SIZE), F32)
    set_parts(pack, 0, feature, (0, 1, 0, 2, 1, 0))
    blank = jnp.zeros((HALF, SIZE), BF16)

    @pl.loop(0, blocks, unroll=4)
    def _(n):
        one = pack[strided(n, HALF, sources), :].astype(BF16)
        low_t[n] = jnp.concatenate([one, blank], axis=0).T
        high_t[n] = jnp.concatenate([blank, one], axis=0).T

    @pl.loop(0, ghosts, unroll=4)
    def _(n):
        one = pack[strided(blocks + 2 * n, HALF, sources), :].astype(BF16)
        other = pack[strided(blocks + 2 * n + 1, HALF, sources), :].astype(BF16)
        twin_t[n] = jnp.concatenate([one, other], axis=0).T

    pack[30 * sources:32 * sources, :] = jnp.zeros((2 * sources, SIZE), F32)
    set_parts(pack, 0, [row * mass for row in feature], (0, 1, 2))

    @pl.loop(0, sources, unroll=8)
    def _(n):
        feat_m[n] = pack[strided(n, 32, sources), :].astype(BF16)

    def set_coefficients(g, r):
        gr = apply_metric(g, r)
        rows = [
            1.0 + gr[0] * r[0] + gr[1] * r[1] + gr[2] * r[2],
            -2.0 * gr[0], -2.0 * gr[1], -2.0 * gr[2],
            g[0], g[1], g[2], 2.0 * g[3], 2.0 * g[4], 2.0 * g[5],
        ]
        set_parts(narrow, 0, rows, (0, 0, 1, 0, 1, 2))
        for t in range(blocks):
            coef[t] = narrow[strided(t, HALF, blocks), :].astype(BF16)

    def units(e):
        local = local_ref[0, e]
        sent = [send_target(KG * e + k) for k in range(KG)]
        ghost, back = blocks + KG * e, blocks + ghosts + KG * e
        return [
            ((e, ghost), (e, ghost + 1)),
            ((sent[0], back), (sent[1], back + 1)),
            ((e, local), (local, e)),
        ]

    def quads(e, kind, unit):
        if kind == 0:
            left = twin_t[e]
        elif kind == 1:
            left = twin_t[blocks + e]
        else:
            left = low_t[unit[0][1]] + high_t[unit[1][1]]
        none = jnp.zeros((HALF, SIZE), BF16)
        top = jnp.concatenate([coef[unit[0][0]], none], axis=1)
        bottom = jnp.concatenate([none, coef[unit[1][0]]], axis=1)
        return dot(left, jnp.concatenate([top, bottom], axis=0))

    def mass_rows(unit):
        one, other = (feat_m[source] for _, source in unit)
        return jnp.concatenate(
            [jnp.concatenate([one, one], axis=1), jnp.concatenate([other, other], axis=1)], axis=0
        )

    def stacked(value):
        return jnp.concatenate(split2(value), axis=0)

    def listed_units(e):
        return [
            (e + step, kind, unit)
            for step in range(STEPS)
            for kind, unit in enumerate(units(e + step))
        ]

    def ahead(listed):
        waiting = []
        for index, item in enumerate(listed):
            waiting.append(quads(*item))
            if index >= AHEAD:
                yield index - AHEAD, listed[index - AHEAD], inverse_of(waiting[index - AHEAD])
        for index in range(max(len(listed) - AHEAD, 0), len(listed)):
            yield index, listed[index], inverse_of(waiting[index])

    def rows_of(block):
        return pl.ds(pl.multiple_of(block * 32, 32), 32)

    def add_sums(into, listed, sums):
        for (e, kind, unit), value in zip(listed, sums):
            one, other = value[0:32, 0:SIZE], value[32:64, SIZE:2 * SIZE]
            if kind == 0:
                into[rows_of(e), :] += one + other
            else:
                into[rows_of(unit[0][0]), :] += one
                into[rows_of(unit[1][0]), :] += other

    def summed(ref, k, count):
        low, middle, high = (ref[strided(k + TERMS * part, count, 32), :] for part in (2, 1, 0))
        return high + (middle + low)

    def place():
        return [src[k * sources:k * sources + blocks, :] for k in range(3)]

    def metric():
        return [own[k * blocks:(k + 1) * blocks, :] for k in range(6)]

    narrow[60 * blocks:, :] = jnp.zeros((4 * blocks, SIZE), F32)

    @pl.loop(0, ITERS)
    def _(iteration):
        g, r = metric(), place()
        set_coefficients(g, r)
        acc[...] = jnp.zeros(acc.shape, F32)

        @pl.loop(0, blocks, step=STEPS)
        def _(e):
            listed = listed_units(e)
            sums = []
            for _, (_, _, unit), inv in ahead(listed):
                sums.append(dot(mass_rows(unit), stacked(inv * inv)))
            add_sums(acc, listed, sums)

        s = [summed(acc, k, blocks) for k in range(TERMS)]
        g, r = metric(), place()
        total = s[0]
        share = 1.0 / total

        def second(i, j, at):
            return (r[i] * r[j] * total - r[i] * s[1 + j] - r[j] * s[1 + i] + s[at]) * share

        spread = [
            second(0, 0, 4) + RIDGE_TERM,
            second(1, 1, 5) + RIDGE_TERM,
            second(2, 2, 6) + RIDGE_TERM,
            second(0, 1, 7),
            second(0, 2, 8),
            second(1, 2, 9),
        ]
        cofactors, determinant = inverse_parts(spread)
        weight = 0.5 * TARGET_SCALE / determinant
        for k in range(6):
            own[k * blocks:(k + 1) * blocks, :] = 0.5 * g[k] + cofactors[k] * weight

    set_coefficients(metric(), place())
    acc[...] = jnp.zeros(acc.shape, F32)
    thirds_acc[...] = jnp.zeros(thirds_acc.shape, F32)

    @pl.loop(0, blocks, step=STEPS)
    def _(e):
        listed = listed_units(e)
        squares, thirds = [], []
        for index, (_, _, unit), inv in ahead(listed):
            square = inv * inv
            cube = stacked(square * inv)
            cubes[3 * e + index] = cube
            left = mass_rows(unit)
            squares.append(dot(left, stacked(square)))
            thirds.append(dot(left, cube))
        add_sums(acc, listed, squares)
        add_sums(thirds_acc, listed, thirds)

    g, r = metric(), place()
    cofactors, determinant = inverse_parts(g)
    volume = jnp.sqrt(determinant) / (SIZE * LISTED)
    density = volume * summed(acc, 0, blocks)
    energy = own[6 * blocks:7 * blocks, :]
    coefficient = (ADIABATIC - 1.0) * energy / density * volume
    scale = 4.0 * src[3 * sources:3 * sources + blocks, :] * coefficient
    own[6 * blocks:7 * blocks, :] = density
    own[7 * blocks:8 * blocks, :] = coefficient
    set_parts(narrow, 0, [scale * row for row in g + apply_metric(g, r) + [jnp.zeros_like(scale)]], (0, 1, 2))
    narrow[30 * blocks:32 * blocks, :] = jnp.zeros((2 * blocks, SIZE), F32)
    for t in range(blocks):
        back_feat[t] = narrow[strided(t, 32, blocks), :].astype(BF16)
    backs[0:32 * blocks, :] = jnp.zeros((32 * blocks, SIZE), F32)

    @pl.loop(0, blocks, step=STEPS)
    def _(e):
        listed = listed_units(e)
        values = []
        for index, (at, kind, unit) in enumerate(listed):
            one, other = (back_feat[target] for target, _ in unit)
            none = jnp.zeros((32, SIZE), BF16)
            left = jnp.concatenate(
                [jnp.concatenate([one, none], axis=1), jnp.concatenate([none, other], axis=1)], axis=0
            )
            value = lax.dot_general(
                left, cubes[3 * e + index], (((1,), (1,)), ((), ())), preferred_element_type=F32
            )
            values.append(value[:, 0:SIZE] + value[:, SIZE:2 * SIZE])
        for (_, kind, unit), value in zip(listed, values):
            for half, (_, source) in enumerate(unit):
                if kind < 2:
                    backs[rows_of(source), :] = value[32 * half:32 * half + 32]
        for (_, kind, unit), value in zip(listed, values):
            for half, (_, source) in enumerate(unit):
                if kind == 2:
                    backs[rows_of(source), :] += value[32 * half:32 * half + 32]

    b = [summed(backs, k, sources) for k in range(9)]
    where = [src[k * sources:(k + 1) * sources, :] for k in range(3)]
    back = [moved - b[6 + k] for k, moved in enumerate(apply_metric(b[0:6], where))]
    f = [summed(thirds_acc, k, blocks) for k in range(4)]
    g, r = metric(), place()
    coefficient = own[7 * blocks:8 * blocks, :]
    forward = apply_metric(g, [r[k] * f[0] - f[1 + k] for k in range(3)])
    for k in range(3):
        pack[k * sources:(k + 1) * sources, :] = back[k]
        narrow[k * blocks:(k + 1) * blocks, :] = 4.0 * coefficient * forward[k] + back[k][0:blocks]
    for t in range(blocks):
        at = slice(t * SIZE, (t + 1) * SIZE)
        final_ref[:, at] = own[strided(t, 6, blocks), :]
        density_ref[:, at] = own[6 * blocks + t:6 * blocks + t + 1, :]
        accel_ref[:, at] = narrow[strided(t, 3, blocks), :]

    for n in range(ghosts):
        pay_ref[4:7, n * SIZE:(n + 1) * SIZE] = pack[strided(blocks + ghosts + n, 3, sources), :]
        slot = tab_ref[c, ghost_row, n]
        pay_ref[0:3, lanes(slot)] = pack[strided(blocks + n, 3, sources), :]


def add_terms(sizes, tab_ref, part_ref, recv_ref, out_ref):
    n_node, capn, capd, blocks = sizes
    c = lax.axis_index("node")
    out_ref[...] = part_ref[...]
    for n in range(blocks * KG):
        past = n - n_node * capn
        row, col = (n % capn, n // capn) if past < 0 else (capn + past // capd, past % capd)
        at = slice(n * SIZE, (n + 1) * SIZE)
        out_ref[:, lanes(tab_ref[c, row, col])] += recv_ref[0:3, at]
    for e in range(blocks):
        at = slice(e * SIZE, (e + 1) * SIZE)
        terms = [recv_ref[4:7, lanes(tab_ref[c, capn + 2, KG * e + k])] for k in range(KG)]
        out_ref[:, at] += sum(terms[1:], terms[0])


def on_device(n_dom, n_node, positions, masses, metric, energy, local_pairs, ghost_pairs, node_sends, domain_sends):
    blocks = local_pairs.shape[0]
    capn, capd = node_sends.shape[2], domain_sends.shape[2]
    ghosts = blocks * KG
    width = blocks * SIZE
    sources = blocks + 2 * ghosts
    slots = n_node + 2
    sizes = (n_node, capn, capd, blocks)
    rows = -(-(capn + 3) // 8) * 8
    vmem = pl.BlockSpec(memory_space=pltpu.VMEM)
    smem = pl.BlockSpec(memory_space=pltpu.SMEM)
    received, tables = pl.pallas_call(
        functools.partial(static_exchange, n_dom, n_node),
        out_shape=(
            jax.ShapeDtypeStruct((slots, 4, width), F32),
            jax.ShapeDtypeStruct((slots, rows, SIZE), jnp.int32),
        ),
        in_specs=[vmem] * 5,
        out_specs=(vmem, vmem),
        scratch_shapes=[
            pltpu.SemaphoreType.DMA((n_node + 1, 2)),
            pltpu.SemaphoreType.DMA((n_node + 1, 2)),
        ],
        compiler_params=pltpu.CompilerParams(collective_id=0, has_side_effects=True),
        name="static_exchange",
    )(positions, masses.reshape(1, width), node_sends.swapaxes(1, 2), domain_sends, ghost_pairs)
    final, density, part, pay = pl.pallas_call(
        functools.partial(compute, sizes),
        out_shape=(
            jax.ShapeDtypeStruct((6, width), F32),
            jax.ShapeDtypeStruct((1, width), F32),
            jax.ShapeDtypeStruct((3, width), F32),
            jax.ShapeDtypeStruct((8, ghosts * SIZE), F32),
        ),
        in_specs=[smem, smem, vmem, vmem, vmem],
        out_specs=(vmem,) * 4,
        scratch_shapes=[
            pltpu.SMEM((slots, ghosts), jnp.int32),
            pltpu.VMEM((4 * sources, SIZE), F32),
            pltpu.VMEM((HALF * sources, SIZE), F32),
            pltpu.VMEM((blocks, SIZE, SIZE), BF16),
            pltpu.VMEM((blocks, SIZE, SIZE), BF16),
            pltpu.VMEM((ghosts, SIZE, SIZE), BF16),
            pltpu.VMEM((sources, 32, SIZE), BF16),
            pltpu.VMEM((HALF * blocks, SIZE), F32),
            pltpu.VMEM((blocks, HALF, SIZE), BF16),
            pltpu.VMEM((32 * blocks, SIZE), F32),
            pltpu.VMEM((32 * blocks, SIZE), F32),
            pltpu.VMEM((3 * blocks, 2 * SIZE, 2 * SIZE), BF16),
            pltpu.VMEM((blocks, 32, SIZE), BF16),
            pltpu.VMEM((32 * sources, SIZE), F32),
            pltpu.VMEM((8 * blocks, SIZE), F32),
        ],
        compiler_params=pltpu.CompilerParams(vmem_limit_bytes=62 * 2**20),
        name="compute",
    )(tables, local_pairs.T, received, metric, energy.reshape(1, width))
    returned = pl.pallas_call(
        functools.partial(term_exchange, n_dom, n_node, capn, capd),
        out_shape=jax.ShapeDtypeStruct((8, ghosts * SIZE), F32),
        in_specs=[vmem],
        out_specs=vmem,
        scratch_shapes=[
            pltpu.SemaphoreType.DMA((n_node + 1,)),
            pltpu.SemaphoreType.DMA((n_node + 1,)),
        ],
        compiler_params=pltpu.CompilerParams(collective_id=1, has_side_effects=True),
        name="term_exchange",
    )(pay)
    accel = pl.pallas_call(
        functools.partial(add_terms, sizes),
        out_shape=jax.ShapeDtypeStruct((3, width), F32),
        in_specs=[smem, vmem, vmem],
        out_specs=vmem,
        name="add_terms",
    )(tables, part, returned)
    return (final, density.reshape(-1), accel)


def solution(mesh):
    in_specs = (
        P(None, ("dom", "node")),
        P(("dom", "node")),
        P(None, ("dom", "node")),
        P(("dom", "node")),
        P(("dom", "node"), None),
        P(("dom", "node"), None),
        P(("dom", "node"), None, None),
        P(("dom", "node"), None, None),
    )
    out_specs = (P(None, ("dom", "node")), P(("dom", "node")), P(None, ("dom", "node")))
    return jax.shard_map(
        functools.partial(on_device, mesh.shape["dom"], mesh.shape["node"]),
        mesh=mesh, in_specs=in_specs, out_specs=out_specs, check_vma=False,
    )
```

time: 418 us -> 43.5 us (0.10)
  the two profiles are of different devices: /device:TPU:26 before, /device:TPU:0 now
where the time goes in v1:
time: 43.5 us; the launch traced here: 43.2 us
  Pallas kernels  42.6 us (98%)
  between operations  0.65 us (1%)
    pallas_call x1, Pallas kernels, on_device(): pl.pallas_call(functools.partial(compute, sizes), out_shape=(jax.ShapeDty...  25.5 us
    pallas_call x1, Pallas kernels, on_device(): pl.pallas_call(functools.partial(static_exchange, n_dom, n_node), out_sha...  8.1 us
    pallas_call x1, Pallas kernels, on_device(): pl.pallas_call(functools.partial(term_exchange, n_dom, n_node, capn, capd...  7.18 us
    pallas_call x1, Pallas kernels, on_device(): pl.pallas_call(functools.partial(add_terms, sizes), out_shape=jax.ShapeDt...  1.86 us

profile of v1, /device:TPU:0, one launch (start us, length us, event | category | flops | bytes accessed | tf_op | source)
XLA Modules:
  0.0 43.2 jit_solution(8964812005591396844)
XLA Ops:
  0.6 8.1 %static_exchange.1 = (f32[6,4,2048]{2,1,0:T(4,128)}, s32[6,8,128]{2,1,0:T(8,128)}) custom-call(f32[3,2048]{1,0:T(4,128)} %pos_ref.1, f32[1,2048]{1,0:T(1,128)} %bitcast.6, s32[1,2,4]{2,1,0:T(2,128)} %bitcast.7, s32[1,2,12]{2,1,0:T(2,128)} %domain_ref.1, s32[1,32]{1,0:T(1,128)} %ghost_ref.1), custom_call_target="tpu_custom_call" | custom-call | tf_op jit(solution)/shard_map/static_exchange/pallas_call | solution.py:519
  8.7 25.5 %compute.1 = (f32[6,2048]{1,0:T(8,128)}, f32[1,2048]{1,0:T(1,128)}, f32[3,2048]{1,0:T(4,128)}, f32[8,4096]{1,0:T(8,128)}) custom-call(s32[6,8,128]{2,1,0:T(8,128)} %get-tuple-element.9.tab_ref, s32[1,16]{1,0:T(1,128)} %bitcast.8, f32[6,4,2048]{2,1,0:T(4,128)} %get-tuple-element.10.recv_ref, f32[6,2048]{1,0:T(8,128)} %metric_ref.1, f32[1,2048]{1,0:T(1,128)} %bitcast.5), custom_call_target="tpu_custom_call" | custom-call | tf_op jit(solution)/shard_map/compute/pallas_call | solution.py:534
  34.2 7.2 %term_exchange.1.recv_ref = f32[8,4096]{1,0:T(8,128)} custom-call(f32[8,4096]{1,0:T(8,128)} %get-tuple-element.14.pay_ref), custom_call_target="tpu_custom_call" | custom-call | tf_op jit(solution)/shard_map/term_exchange/pallas_call | solution.py:564
  41.4 1.9 %add_terms.1 = f32[3,2048]{1,0:T(4,128)} custom-call(s32[6,8,128]{2,1,0:T(8,128)} %get-tuple-element.9.tab_ref, f32[3,2048]{1,0:T(4,128)} %get-tuple-element.13.part_ref, f32[8,4096]{1,0:T(8,128)} %term_exchange.1.recv_ref), custom_call_target="tpu_custom_call" | custom-call | tf_op jit(solution)/shard_map/add_terms/pallas_call | solution.py:576

commit v2 on v1

--- a/solution.py
+++ b/solution.py
@@ -11,8 +11,8 @@
 KG = 2
 LISTED = 3
 ITERS = 3
-STEPS = 8
-AHEAD = 2
+STEPS = 16
+AHEAD = 4
 ADIABATIC = 5.0 / 3.0
 TARGET_SCALE = 0.5
 RIDGE_TERM = 0.1
@@ -48,41 +48,39 @@
 
 
 def static_exchange(
-    n_dom, n_node, pos_ref, mass_ref, node_ref, domain_ref, ghost_ref, recv_ref, rtab_ref, send, land
+    n_dom, n_node, pos_ref, mass_ref, node_ref, domain_ref, ghost_ref, recv_ref, rmass_ref, rtab_ref,
+    tab, none, no_tab, send, land, local,
 ):
     a, c = lax.axis_index("dom"), lax.axis_index("node")
     prev_slot, next_slot = n_node, n_node + 1
-    recv_ref[c, 0:3, :] = pos_ref[...]
-    recv_ref[c, 3:4, :] = mass_ref[...]
-    rtab_ref[c] = jnp.zeros(rtab_ref.shape[1:], jnp.int32)
     capn = node_ref.shape[1]
-    rtab_ref[c, 0:capn, 0:n_node] = node_ref[0]
-    rtab_ref[c, capn:capn + 2, 0:domain_ref.shape[2]] = domain_ref[0]
-    rtab_ref[c, capn + 2:capn + 3, 0:ghost_ref.shape[1]] = ghost_ref[...]
-
-    @pl.when(a == 0)
-    def _():
-        recv_ref[prev_slot] = jnp.zeros(recv_ref.shape[1:], F32)
-        rtab_ref[prev_slot] = jnp.zeros(rtab_ref.shape[1:], jnp.int32)
-
-    @pl.when(a == n_dom - 1)
-    def _():
-        recv_ref[next_slot] = jnp.zeros(recv_ref.shape[1:], F32)
-        rtab_ref[next_slot] = jnp.zeros(rtab_ref.shape[1:], jnp.int32)
-
+    none[...] = jnp.zeros(none.shape, F32)
+    no_tab[...] = jnp.zeros(no_tab.shape, jnp.int32)
+    tab[...] = jnp.zeros(tab.shape, jnp.int32)
+    tab[0:capn, 0:n_node] = node_ref[0]
+    tab[capn:capn + 2, 0:domain_ref.shape[2]] = domain_ref[0]
+    tab[capn + 2:capn + 3, 0:ghost_ref.shape[1]] = ghost_ref[...]
     greet(n_dom, n_node)
+    parts = ((pos_ref, recv_ref), (mass_ref, rmass_ref), (tab, rtab_ref))
 
     def copies(lane, target, slot):
         return [
             pltpu.make_async_remote_copy(
-                src_ref=ref.at[c],
-                dst_ref=ref.at[slot],
+                src_ref=src,
+                dst_ref=dst.at[slot],
                 send_sem=send.at[lane, part],
                 recv_sem=land.at[lane, part],
                 device_id=target,
                 device_id_type=MESH,
             )
-            for part, ref in enumerate((recv_ref, rtab_ref))
+            for part, (src, dst) in enumerate(parts)
+        ]
+
+    def blanks(lane, slot):
+        return [
+            pltpu.make_async_copy(none, recv_ref.at[slot], local.at[lane, 0]),
+            pltpu.make_async_copy(none.at[0:1], rmass_ref.at[slot], local.at[lane, 1]),
+            pltpu.make_async_copy(no_tab, rtab_ref.at[slot], local.at[lane, 2]),
         ]
 
     to_prev = copies(0, (a - 1, c), next_slot)
@@ -90,10 +88,18 @@
     around = [
         copies(1 + turn, (a, lax.rem(c + turn, n_node)), c) for turn in range(1, n_node)
     ]
-    finish(a, n_dom, to_prev, to_next, around)
-
-
-def finish(a, n_dom, to_prev, to_next, around):
+    own = [
+        pltpu.make_async_copy(src, dst.at[c], local.at[0, part])
+        for part, (src, dst) in enumerate(parts)
+    ]
+    finish(a, n_dom, to_prev, to_next, around, own, blanks(1, prev_slot), blanks(2, next_slot))
+
+
+def finish(a, n_dom, to_prev, to_next, around, own, prev_blank, next_blank):
+    def each(copies, act):
+        for copy in copies:
+            getattr(copy, act)()
+
     @pl.when(a > 0)
     def _():
         for copy in to_prev:
@@ -105,11 +111,22 @@
             copy.start()
 
     for group in around:
-        for copy in group:
-            copy.start()
+        each(group, "start")
+    each(own, "start")
+
+    @pl.when(a == 0)
+    def _():
+        each(prev_blank, "start")
+        each(prev_blank, "wait")
+
+    @pl.when(a == n_dom - 1)
+    def _():
+        each(next_blank, "start")
+        each(next_blank, "wait")
+
+    each(own, "wait")
     for group in around:
-        for copy in group:
-            copy.wait()
+        each(group, "wait")
 
     @pl.when(a > 0)
     def _():
@@ -126,21 +143,11 @@
             copy.wait_recv()
 
 
-def term_exchange(n_dom, n_node, capn, capd, pay_ref, recv_ref, send, land):
+def term_exchange(n_dom, n_node, capn, capd, pay_ref, recv_ref, send, land, local):
     a, c = lax.axis_index("dom"), lax.axis_index("node")
     first = n_node * capn
     prev_cols = pl.ds(first * SIZE, capd * SIZE)
     next_cols = pl.ds((first + capd) * SIZE, capd * SIZE)
-    recv_ref[:, lanes(c * capn, capn)] = pay_ref[:, lanes(c * capn, capn)]
-
-    @pl.when(a == 0)
-    def _():
-        recv_ref[:, prev_cols] = jnp.zeros((8, capd * SIZE), F32)
-
-    @pl.when(a == n_dom - 1)
-    def _():
-        recv_ref[:, next_cols] = jnp.zeros((8, capd * SIZE), F32)
-
     greet(n_dom, n_node)
 
     def copies(lane, target, src, dst):
@@ -161,7 +168,12 @@
     for turn in range(1, n_node):
         peer = lax.rem(c + turn, n_node)
         around.append(copies(1 + turn, (a, peer), lanes(peer * capn, capn), lanes(c * capn, capn)))
-    finish(a, n_dom, to_prev, to_next, around)
+
+    def kept(lane, cols):
+        return [pltpu.make_async_copy(pay_ref.at[:, cols], recv_ref.at[:, cols], local.at[lane])]
+
+    own = kept(0, lanes(c * capn, capn))
+    finish(a, n_dom, to_prev, to_next, around, own, kept(1, prev_cols), kept(2, next_cols))
 
 
 def set_parts(out, base, values, order):
@@ -210,8 +222,8 @@
 
 
 def compute(
-    sizes,
-    tab_ref, local_ref, recv_ref, metric_ref, energy_ref,
+    n_dom, sizes,
+    tab_ref, local_ref, recv_ref, rmass_ref, metric_ref, energy_ref,
     final_ref, density_ref, accel_ref, pay_ref,
     held, src, pack, low_t, high_t, twin_t, feat_m, narrow, coef, acc, thirds_acc, cubes, back_feat, backs, own,
 ):
@@ -226,6 +238,10 @@
     def strided(n, count, stride):
         return pl.ds(n, count, stride=stride)
 
+    def put_source(n, slot, at):
+        src[strided(n, 3, sources), :] = recv_ref[slot, :, at]
+        src[3 * sources + n:3 * sources + n + 1, :] = rmass_ref[slot, :, at]
+
     for slot in range(slots):
         if slot >= n_node:
             @pl.loop(0, ghosts, unroll=8)
@@ -238,7 +254,7 @@
 
     for n in range(blocks):
         at = slice(n * SIZE, (n + 1) * SIZE)
-        src[strided(n, 4, sources), :] = recv_ref[c, :, at]
+        put_source(n, c, at)
         own[strided(n, 6, blocks), :] = metric_ref[:, at]
         own[6 * blocks + n:6 * blocks + n + 1, :] = energy_ref[:, at]
 
@@ -251,7 +267,7 @@
         row = jnp.where(near, slot % capn, jnp.where(low, capn + 1, capn))
         col = jnp.where(near, c, jnp.where(low, past, past - capd))
         block = tab_ref[from_slot, row, col]
-        src[strided(blocks + n, 4, sources), :] = recv_ref[from_slot, :, lanes(block)]
+        put_source(blocks + n, from_slot, lanes(block))
 
     for n in range(ghosts):
         if n < first:
@@ -261,7 +277,7 @@
         else:
             from_slot, there = n_node + 1, n - capd
         block = held[from_slot, there]
-        src[strided(blocks + ghosts + n, 4, sources), :] = recv_ref[from_slot, :, lanes(block)]
+        put_source(blocks + ghosts + n, from_slot, lanes(block))
 
     def send_target(n):
         near = n < first
@@ -489,6 +505,16 @@
         slot = tab_ref[c, ghost_row, n]
         pay_ref[0:3, lanes(slot)] = pack[strided(blocks + n, 3, sources), :]
 
+    a = lax.axis_index("dom")
+
+    @pl.when(a == 0)
+    def _():
+        pay_ref[:, first * SIZE:(first + capd) * SIZE] = jnp.zeros((8, capd * SIZE), F32)
+
+    @pl.when(a == n_dom - 1)
+    def _():
+        pay_ref[:, (first + capd) * SIZE:ghosts * SIZE] = jnp.zeros((8, capd * SIZE), F32)
+
 
 def add_terms(sizes, tab_ref, part_ref, recv_ref, out_ref):
     n_node, capn, capd, blocks = sizes
@@ -516,30 +542,36 @@
     rows = -(-(capn + 3) // 8) * 8
     vmem = pl.BlockSpec(memory_space=pltpu.VMEM)
     smem = pl.BlockSpec(memory_space=pltpu.SMEM)
-    received, tables = pl.pallas_call(
+    anywhere = pl.BlockSpec(memory_space=pl.ANY)
+    received, rmass, tables = pl.pallas_call(
         functools.partial(static_exchange, n_dom, n_node),
         out_shape=(
-            jax.ShapeDtypeStruct((slots, 4, width), F32),
+            jax.ShapeDtypeStruct((slots, 3, width), F32),
+            jax.ShapeDtypeStruct((slots, 1, width), F32),
             jax.ShapeDtypeStruct((slots, rows, SIZE), jnp.int32),
         ),
-        in_specs=[vmem] * 5,
-        out_specs=(vmem, vmem),
+        in_specs=[anywhere] * 2 + [vmem] * 3,
+        out_specs=(anywhere,) * 3,
         scratch_shapes=[
-            pltpu.SemaphoreType.DMA((n_node + 1, 2)),
-            pltpu.SemaphoreType.DMA((n_node + 1, 2)),
+            pltpu.VMEM((rows, SIZE), jnp.int32),
+            pltpu.VMEM((3, width), F32),
+            pltpu.VMEM((rows, SIZE), jnp.int32),
+            pltpu.SemaphoreType.DMA((n_node + 1, 3)),
+            pltpu.SemaphoreType.DMA((n_node + 1, 3)),
+            pltpu.SemaphoreType.DMA((3, 3)),
         ],
         compiler_params=pltpu.CompilerParams(collective_id=0, has_side_effects=True),
         name="static_exchange",
     )(positions, masses.reshape(1, width), node_sends.swapaxes(1, 2), domain_sends, ghost_pairs)
     final, density, part, pay = pl.pallas_call(
-        functools.partial(compute, sizes),
+        functools.partial(compute, n_dom, sizes),
         out_shape=(
             jax.ShapeDtypeStruct((6, width), F32),
             jax.ShapeDtypeStruct((1, width), F32),
             jax.ShapeDtypeStruct((3, width), F32),
             jax.ShapeDtypeStruct((8, ghosts * SIZE), F32),
         ),
-        in_specs=[smem, smem, vmem, vmem, vmem],
+        in_specs=[smem, smem, vmem, vmem, vmem, vmem],
         out_specs=(vmem,) * 4,
         scratch_shapes=[
             pltpu.SMEM((slots, ghosts), jnp.int32),
@@ -560,15 +592,16 @@
         ],
         compiler_params=pltpu.CompilerParams(vmem_limit_bytes=62 * 2**20),
         name="compute",
-    )(tables, local_pairs.T, received, metric, energy.reshape(1, width))
+    )(tables, local_pairs.T, received, rmass, metric, energy.reshape(1, width))
     returned = pl.pallas_call(
         functools.partial(term_exchange, n_dom, n_node, capn, capd),
         out_shape=jax.ShapeDtypeStruct((8, ghosts * SIZE), F32),
-        in_specs=[vmem],
-        out_specs=vmem,
+        in_specs=[anywhere],
+        out_specs=anywhere,
         scratch_shapes=[
             pltpu.SemaphoreType.DMA((n_node + 1,)),
             pltpu.SemaphoreType.DMA((n_node + 1,)),
+            pltpu.SemaphoreType.DMA((3,)),
         ],
         compiler_params=pltpu.CompilerParams(collective_id=1, has_side_effects=True),
         name="term_exchange",

time: 43.5 us -> 37.1 us (0.85)
  Pallas kernels: 42.6 us -> 36.2 us
    pallas_call x1, Pallas kernels: 25.5 us -> 20.2 us  [on_device(): pl.pallas_call(functools.partial(compute, n_dom, sizes), out_shape=(jax.S...]
    pallas_call x1, Pallas kernels: 7.18 us -> 6.31 us  [on_device(): pl.pallas_call(functools.partial(term_exchange, n_dom, n_node, capn, capd...]
where the time goes in v2:
time: 37.1 us; the launch traced here: 36.9 us
  Pallas kernels  36.2 us (98%)
  between operations  0.65 us (2%)
    pallas_call x1, Pallas kernels, on_device(): pl.pallas_call(functools.partial(compute, n_dom, sizes), out_shape=(jax.S...  20.2 us
    pallas_call x1, Pallas kernels, on_device(): pl.pallas_call(functools.partial(static_exchange, n_dom, n_node), out_sha...  7.9 us
    pallas_call x1, Pallas kernels, on_device(): pl.pallas_call(functools.partial(term_exchange, n_dom, n_node, capn, capd...  6.31 us
    pallas_call x1, Pallas kernels, on_device(): pl.pallas_call(functools.partial(add_terms, sizes), out_shape=jax.ShapeDt...  1.86 us

profile of v2, /device:TPU:0, one launch (start us, length us, event | category | flops | bytes accessed | tf_op | source)
XLA Modules:
  0.0 36.9 jit_solution(16496665033141160283)
XLA Ops:
  0.6 7.9 %static_exchange.1 = (f32[6,3,2048]{2,1,0:T(4,128)}, f32[6,1,2048]{2,1,0:T(1,128)}, s32[6,8,128]{2,1,0:T(8,128)}) custom-call(f32[3,2048]{1,0:T(4,128)} %pos_ref.1, f32[1,2048]{1,0:T(1,128)} %bitcast.6, s32[1,2,4]{2,1,0:T(2,128)} %bitcast.7, s32[1,2,12]{2,1,0:T(2,128)} %domain_ref.1, s32[1,32]{1,0:T(1,128)} %ghost_ref.1), custom_call_target="tpu_custom_call" | custom-call | tf_op jit(solution)/shard_map/static_exchange/pallas_call | solution.py:546
  8.5 20.2 %compute.1 = (f32[6,2048]{1,0:T(8,128)}, f32[1,2048]{1,0:T(1,128)}, f32[3,2048]{1,0:T(4,128)}, f32[8,4096]{1,0:T(8,128)}) custom-call(s32[6,8,128]{2,1,0:T(8,128)} %get-tuple-element.10.tab_ref, s32[1,16]{1,0:T(1,128)} %bitcast.8, f32[6,3,2048]{2,1,0:T(4,128)} %get-tuple-element.11.recv_ref, f32[6,1,2048]{2,1,0:T(1,128)} %get-tuple-element.12.rmass_ref, ...), custom_call_target="tpu_custom_call" | custom-call | tf_op jit(solution)/shard_map/compute/pallas_call | solution.py:566
  28.7 6.3 %term_exchange.1.recv_ref = f32[8,4096]{1,0:T(8,128)} custom-call(f32[8,4096]{1,0:T(8,128)} %get-tuple-element.16.pay_ref), custom_call_target="tpu_custom_call" | custom-call | tf_op jit(solution)/shard_map/term_exchange/pallas_call | solution.py:596
  35.0 1.9 %add_terms.1 = f32[3,2048]{1,0:T(4,128)} custom-call(s32[6,8,128]{2,1,0:T(8,128)} %get-tuple-element.10.tab_ref, f32[3,2048]{1,0:T(4,128)} %get-tuple-element.15.part_ref, f32[8,4096]{1,0:T(8,128)} %term_exchange.1.recv_ref), custom_call_target="tpu_custom_call" | custom-call | tf_op jit(solution)/shard_map/add_terms/pallas_call | solution.py:609
